TPU v7x, 512 devices: a whole 4x8x8 slice. The times are simulated.
512 devices in a mesh: ia: 4 (over z_hi), ja: 16 (over z_lo, y), ka: 8 (over x, core).
Axes of the slice: x: 4, y: 8, z: 8 (z_hi: 4, z_lo: 2; z = z_hi * 2 + z_lo), core: 2. Of those that a mesh axis runs over, the one named last changes fastest.
Arguments:
- tensor: float32 [32, 2048, 4096], P('ka', 'ia', 'ja'), may hold values from -6 to 6
- factor_b: float32 [4096, 64], P(('ja', 'ka')), may hold values from -0.09375 to 0.09375
- factor_c: float32 [32, 64], P('ka'), may hold values from -1 to 1
Outputs:
- update: float32 [2048, 64], P(('ia', 'ja', 'ka'))
All inputs are finite; a program needn't handle non-finite values.
Results may differ from a plain program's by a relative error of at most 0.00011.
Values sent between devices are 32-bit elements; how exact they have to be, the bound alone decides.
No kernel may reach another device: no remote copies, remote signals or barrier semaphores. Data moves between devices by JAX's collectives and lax.ppermute only.
A program may use at most 64 MiB of HBM per device.

v0:
```python
import jax
import jax.numpy as jnp
from jax import lax
from jax.sharding import PartitionSpec as P


def per_device(tensor, factor_b, factor_c):
    partial_value = jnp.einsum(
        "kij,jr->kir",
        tensor,
        lax.all_gather(factor_b, "ka", axis=0, tiled=True),
        precision=lax.Precision.HIGHEST,
    )
    local_sums = jnp.einsum("kir,kr->ir", partial_value, factor_c, precision=lax.Precision.HIGHEST)
    local_gram_b = jnp.dot(
        factor_b.T, factor_b, precision=lax.Precision.HIGHEST, preferred_element_type=jnp.float32
    )
    local_gram_c = jnp.dot(
        factor_c.T, factor_c, precision=lax.Precision.HIGHEST, preferred_element_type=jnp.float32
    )
    gram_b = lax.psum(local_gram_b, ("ja", "ka"))
    gram_c = lax.psum(local_gram_c, "ka")
    owned = lax.psum_scatter(local_sums, ("ja", "ka"), scatter_dimension=0, tiled=True)
    gram = gram_b * gram_c
    lower = jnp.linalg.cholesky(gram)
    solved = jax.scipy.linalg.cho_solve((lower, True), owned.T)
    return solved.T


def solution(mesh):
    in_specs = (P("ka", "ia", "ja"), P(("ja", "ka"), None), P("ka", None))
    out_specs = P(("ia", "ja", "ka"), None)
    return jax.shard_map(
        per_device, mesh=mesh, in_specs=in_specs, out_specs=out_specs, check_vma=False
    )
```

profile of v0, /device:TPU:1, one launch (start us, length us, event | category | flops | bytes accessed | tf_op | source)
XLA Modules:
  0.0 976.3 jit_solution(13038293360370362901)
XLA Ops:
  6.5 0.0 copy-start
  6.5 0.0 copy-start.1
  6.5 0.0 copy-start.2
  6.5 0.0 all-reduce.3.cloned.1.call-start
  6.5 19.8 %all_gather.3 = f32[256,64]{1,0:T(8,128)S(1)} all-gather(f32[32,64]{1,0:T(8,128)} %param.4), channel_id=1, replica_groups=mesh['ia'=4,'ja'=16,'ka'=8] {'ka'}, dimensions={0}, use_global_device_ids=true | all-gather | bytes 73728 | tf_op jit(solution)/shard_map/all_gather | solution.py:11
  26.3 0.0 copy-done
  26.4 2.5 fusion.1
  28.9 0.8 copy.18
  29.6 0.0 all-reduce.3.cloned.1.call-update
  29.7 0.0 copy-done.1
  29.7 0.2 fusion.11
  29.9 0.0 copy-done.2
  29.9 0.2 fusion.12
  30.2 544.1 %psum.14 = f32[64,64]{0,1:T(8,128)S(1)} all-reduce(f32[64,64]{0,1:T(8,128)S(1)} %fusion.11), channel_id=1, replica_groups=mesh['ia'=4,'ja'=16,'ka'=8] {'ja','ka'}, use_global_device_ids=true, to_apply=%region_0.0 | all-reduce | flops 4096 | bytes 32768 | tf_op jit(solution)/shard_map/psum | solution.py:21
  574.2 26.6 %psum.15 = f32[64,64]{0,1:T(8,128)S(1)} all-reduce(f32[64,64]{0,1:T(8,128)S(1)} %fusion.12), channel_id=1, replica_groups=mesh['ia'=4,'ja'=16,'ka'=8] {'ka'}, use_global_device_ids=true, to_apply=%region_1.0 | all-reduce | flops 4096 | bytes 32768 | tf_op jit(solution)/shard_map/psum | solution.py:22
  600.8 0.1 copy.9
  600.9 5.8 cholesky.16
  606.8 0.6 compare_reduce_fusion
  607.4 0.7 fusion.3
  608.1 4.9 custom-call.10
  613.0 1.3 dynamic-slice
  614.9 352.8 %all-reduce.3.cloned.1.call-done = f32[512,64]{0,1:T(8,128)} async-done(((f32[512,64]{0,1:T(8,128)}), f32[512,64]{0,1:T(8,128)}) %all-reduce.3.cloned.1.call-update) | async-done | bytes 131088
  967.7 1.0 fusion.4
  968.7 0.8 fusion.6
  (3 shorter events, 0.0 us)
Async XLA Ops:
  6.5 19.8 %copy-start = (f32[4,512,256]{2,1,0:T(8,128)S(1)}, f32[4,512,256]{2,1,0:T(8,128)}, u32[]{:S(2)}) copy-start(f32[4,512,256]{2,1,0:T(8,128)} %param.3) | copy-start | bytes 6291460
  6.5 23.1 %copy-start.1 = (f32[32,64]{1,0:T(8,128)S(1)}, f32[32,64]{1,0:T(8,128)}, u32[]{:S(2)}) copy-start(f32[32,64]{1,0:T(8,128)} %param.4) | copy-start | bytes 24580
  6.5 23.4 %copy-start.2 = (f32[4,64]{1,0:T(4,128)S(1)}, f32[4,64]{1,0:T(4,128)}, u32[]{:S(2)}) copy-start(f32[4,64]{1,0:T(4,128)} %param.5) | copy-start | bytes 3076
  6.5 961.1 %all-reduce.3.cloned.1.call-start = ((), (), s32[]{:S(2)}) async-start(), calls=%async_computation | async-start | bytes 262144
Sparse Core Ops, SparseCore 0:
  29.8 937.8 all-reduce.2
where the time goes:
time: 977 us; the launch traced here: 976 us
  blocking collectives  590 us (60%)
  waiting for transfers between devices  353 us (36%)
  between operations  14.1 us (1%)
  other arithmetic  12.1 us (1%)
    psum x1, blocking collectives, per_device(): gram_b = lax.psum(local_gram_b, ('ja', 'ka'))  544 us
    unnamed x2, waiting for transfers between devices  353 us
    psum x1, blocking collectives, per_device(): gram_c = lax.psum(local_gram_c, 'ka')  26.6 us
    all_gather x1, blocking collectives, per_device(): lax.all_gather(factor_b, 'ka', axis=0, tiled=True)  19.8 us
  transfers between devices with their start and end apart: 1, of which 1 were waited for; matrix products, arithmetic and copies ran while one was open for 1% of the time, Pallas kernels for 0%

commit v1 on v0

v1 whole, which is shorter than its diff:
```python
import jax
import jax.numpy as jnp
from jax import lax
from jax.sharding import PartitionSpec as P

HI = lax.Precision.HIGHEST


def per_device(tensor, factor_b, factor_c):
    n_ja, n_ka = lax.axis_size("ja"), lax.axis_size("ka")
    rows_b, rank = factor_b.shape
    depth = factor_c.shape[0]
    mine = jnp.concatenate([factor_b, factor_c], axis=0)
    block = lax.all_to_all(
        jnp.broadcast_to(mine[None], (n_ka,) + mine.shape), "ka", 0, 0, tiled=True
    )
    b_block = block[:, :rows_b].reshape(n_ka * rows_b, rank)
    c_all = block[:, rows_b:].reshape(n_ka * depth, rank)
    partial_value = jnp.einsum("kij,jr->kir", tensor, b_block, precision=HI)
    local_sums = jnp.einsum("kir,kr->ir", partial_value, factor_c, precision=HI)
    gram = jnp.dot(b_block.T, b_block, precision=HI) * jnp.dot(c_all.T, c_all, precision=HI)
    peers = n_ja * n_ka
    sums_part = local_sums.reshape(peers, -1)
    piece = rank // n_ka
    gram_part = lax.dynamic_slice_in_dim(gram, lax.axis_index("ka") * piece, piece, 0)
    gram_part = jnp.broadcast_to(gram_part.reshape(1, -1), (peers, piece * rank))
    got = lax.all_to_all(
        jnp.concatenate([sums_part, gram_part], axis=1), ("ja", "ka"), 0, 0, tiled=True
    )
    owned = jnp.sum(got[:, : sums_part.shape[1]], axis=0).reshape(-1, rank)
    gram = jnp.sum(got[:, sums_part.shape[1] :].reshape(n_ja, n_ka, -1), axis=0).reshape(rank, rank)
    lower = jnp.linalg.cholesky(gram)
    solved = jax.scipy.linalg.cho_solve((lower, True), owned.T)
    return solved.T


def solution(mesh):
    in_specs = (P("ka", "ia", "ja"), P(("ja", "ka"), None), P("ka", None))
    out_specs = P(("ia", "ja", "ka"), None)
    return jax.shard_map(
        per_device, mesh=mesh, in_specs=in_specs, out_specs=out_specs, check_vma=False
    )
```

time: 977 us -> 60.7 us (0.06)
  blocking collectives: 590 us -> 24.9 us
  waiting for transfers between devices: 353 us -> 4.9 us
  between operations: 14.1 us -> 0.12 us
  starting transfers between devices: 0.01 us -> 10.1 us
    psum x2 -> x0, blocking collectives: 571 us -> none  [the longest x1 544 us: per_device(): gram_b = lax.psum(local_gram_b, ('ja', 'ka'))]
    unnamed x2 -> x0, waiting for transfers between devices: 353 us -> none
    all_to_all x0 -> x1, blocking collectives: none -> 24.9 us  [per_device(): lax.all_to_all(jnp.concatenate([sums_part, gram_part], axis=1), ('ja', 'k...]
    all_gather x1 -> x0, blocking collectives: 19.8 us -> none  [per_device(): lax.all_gather(factor_b, 'ka', axis=0, tiled=True)]
    all_to_all x0 -> x1, starting transfers between devices: none -> 10.1 us  [per_device(): lax.all_to_all(jnp.broadcast_to(mine[None], (n_ka,) + mine.shape), 'ka',...]
  transfers between devices with their start and end apart: 1 -> 1, of which waited for: 1 -> 1; matrix products, arithmetic and copies ran while one was open for 1% -> 0% of each run, Pallas kernels for 0% -> 0%
where the time goes in v1:
time: 60.7 us; the launch traced here: 60.4 us
  blocking collectives  24.9 us (41%)
  other arithmetic  13.9 us (23%)
  starting transfers between devices  10.1 us (17%)
  waiting for transfers between devices  4.9 us (8%)
  matrix products  4.21 us (7%)
  local copies, waits for them, and re-layouts  2.24 us (4%)
    all_to_all x1, blocking collectives, per_device(): lax.all_to_all(jnp.concatenate([sums_part, gram_part], axis=1), ('ja', 'k...  24.9 us
    all_to_all x1, starting transfers between devices, per_device(): lax.all_to_all(jnp.broadcast_to(mine[None], (n_ka,) + mine.shape), 'ka',...  10.1 us
    another operation x3, other arithmetic, per_device(): lower = jnp.linalg.cholesky(gram)  6.52 us
    another operation x2, other arithmetic, per_device(): solved = jax.scipy.linalg.cho_solve((lower, True), owned.T)  5.55 us
    all_to_all x1, waiting for transfers between devices, per_device(): lax.all_to_all(jnp.broadcast_to(mine[None], (n_ka,) + mine.shape), 'ka',...  4.9 us
    dot_general x1, matrix products, per_device(): partial_value = jnp.einsum('kij,jr->kir', tensor, b_block, precision=HI)  2.68 us
  transfers between devices with their start and end apart: 1, of which 1 were waited for; matrix products, arithmetic and copies ran while one was open for 0% of the time, Pallas kernels for 0%

profile of v1, /device:TPU:1, one launch (start us, length us, event | category | flops | bytes accessed | tf_op | source)
XLA Modules:
  0.0 60.4 jit_solution(9560775018314292620)
XLA Ops:
  0.0 0.0 copy-start
  0.0 0.9 %pad_maximum_fusion.1 = f32[36,64]{1,0:T(8,128)S(1)} fusion(f32[4,64]{1,0:T(4,128)} %param.5, f32[32,64]{1,0:T(8,128)} %param.4), kind=kLoop, calls=%fused_computation.20 | loop fusion | flops 2304 | bytes 18432 | tf_op jit(solution)/shard_map/concatenate | solution.py:13
  0.9 0.8 %reshape.45 = f32[8,1,2304]{2,1,0:T(1,128)} reshape(f32[8,36,64]{2,1,0:T(8,128)S(1)} %broadcast_in_dim.7) | data formatting | bytes 147456
  1.7 10.1 %all-to-all-start = ((f32[8,1,2304]{2,1,0:T(1,128)}), f32[8,1,2304]{2,1,0:T(1,128)S(1)}, u32[]{:S(2)}, u32[]{:S(2)}) async-start(f32[8,1,2304]{2,1,0:T(1,128)} %reshape.45), calls=%async_computation | async-start | bytes 147456 | tf_op jit(solution)/shard_map/all_to_all | solution.py:14
  11.8 4.9 %all-to-all-done = f32[8,1,2304]{2,1,0:T(1,128)S(1)} async-done(((f32[8,1,2304]{2,1,0:T(1,128)}), f32[8,1,2304]{2,1,0:T(1,128)S(1)}, u32[]{:S(2)}, u32[]{:S(2)}) %all-to-all-start) | async-done | bytes 73760 | tf_op jit(solution)/shard_map/all_to_all | solution.py:14
  16.7 0.5 broadcast.76
  17.2 0.8 %reduce.8 = f32[8,2304]{1,0:T(8,128)S(1)} reduce(f32[8,1,2304]{2,1,0:T(1,128)S(1)} %all-to-all-done, f32[]{:T(128)} %broadcast.76), dimensions={1}, to_apply=%all_to_all.11.reduce_sub_computation | reduce | bytes 147460 | tf_op jit(solution)/shard_map/all_to_all | solution.py:14
  18.0 0.1 reshape.46
  18.1 0.4 convolution_bitcast_fusion.1
  18.5 0.2 convolution_bitcast_fusion
  18.8 0.1 reshape.44
  18.9 0.0 copy-done
  18.9 2.7 %fusion = f32[64,512]{1,0:T(8,128)S(1)} fusion(f32[256,64,1]{1,0,2:T(8,128)S(1)} %bitcast.37, f32[4,512,256]{2,1,0:T(8,128)S(1)} %copy-done, f32[64,4]{0,1:T(4,128)} %bitcast.38), kind=kOutput, calls=%fused_computation.1 | convolution fusion | flops 402882560 | bytes 2294784 | tf_op jit(solution)/shard_map/kij,jr->kir/dot_general | solution.py:19
  21.6 0.1 copy.21
  21.7 0.1 reshape.35
  21.9 0.3 all_to_all.12
  22.1 24.9 %all_to_all.17 = f32[128,1,768]{2,1,0:T(1,128)S(1)} all-to-all(f32[128,1,768]{2,1,0:T(1,128)S(1)} %all_to_all.12), channel_id=1, replica_groups=mesh['ia'=4,'ja'=16,'ka'=8] {'ja','ka'}, dimensions={0} | all-to-all | bytes 786432 | tf_op jit(solution)/shard_map/all_to_all | solution.py:27
  47.1 0.1 reshape.38
  47.2 0.1 reshape.37
  47.3 0.1 copy.13
  47.4 5.8 %cholesky.16 = f32[64,64]{1,0:T(8,128)S(1)} custom-call(f32[64,64]{1,0:T(8,128)S(1)} %fusion.7), custom_call_target="Cholesky" | custom-call | tf_op jit(solution)/shard_map/jit(cholesky)/cholesky | solution.py:32
  53.3 0.6 %compare_reduce_fusion = pred[]{:T(512)} fusion(f32[64]{0:T(128)S(1)} %select_reduce_fusion), kind=kLoop, calls=%fused_computation.23 | loop fusion | flops 127 | bytes 257 | tf_op jit(solution)/shard_map/jit(cholesky)/cholesky | solution.py:32
  53.9 0.7 %fusion.2 = f32[1,64,64]{2,1,0:T(8,128)S(1)} fusion(f32[64,64]{1,0:T(8,128)S(1)} %cholesky.16, pred[]{:T(512)} %compare_reduce_fusion), kind=kLoop, calls=%fused_computation.10 | loop fusion | flops 16384 | bytes 32769 | tf_op jit(solution)/shard_map/jit(_cho_solve)/triangular_solve | solution.py:33
  54.6 4.9 %custom-call.10 = f32[1,64,64]{1,2,0:T(8,128)S(1)} custom-call(f32[1,64,64]{2,1,0:T(8,128)S(1)} %fusion.2), custom_call_target="InvertDiagBlocksLowerTriangular" | custom-call | tf_op jit(solution)/shard_map/jit(_cho_solve)/triangular_solve | solution.py:33
  59.5 0.2 fusion.5
  59.6 0.8 %fusion.3 = f32[4,64]{1,0:T(4,128)} fusion(f32[64,4]{0,1:T(4,128)S(1)} %fusion.5, f32[1,64,64]{1,2,0:T(8,128)S(1)} %custom-call.10), kind=kOutput, calls=%fused_computation.11 | convolution fusion | flops 196608 | bytes 18432 | tf_op jit(solution)/shard_map/jit(_cho_solve)/triangular_solve | solution.py:33
  (10 shorter events, 0.2 us)
Async XLA Ops:
  0.0 18.9 %copy-start = (f32[4,512,256]{2,1,0:T(8,128)S(1)}, f32[4,512,256]{2,1,0:T(8,128)}, u32[]{:S(2)}) copy-start(f32[4,512,256]{2,1,0:T(8,128)} %param.3) | copy-start | bytes 6291460
  1.7 15.0 %all-to-all-start = ((f32[8,1,2304]{2,1,0:T(1,128)}), f32[8,1,2304]{2,1,0:T(1,128)S(1)}, u32[]{:S(2)}, u32[]{:S(2)}) async-start(f32[8,1,2304]{2,1,0:T(1,128)} %reshape.45), calls=%async_computation | async-start | bytes 147456 | tf_op jit(solution)/shard_map/all_to_all | solution.py:14

commit v2 on v1

v2 whole, which is shorter than its diff:
```python
import functools

import jax
import jax.numpy as jnp
from jax import lax
from jax.experimental import pallas as pl
from jax.experimental.pallas import tpu as pltpu
from jax.sharding import PartitionSpec as P

HI = lax.Precision.HIGHEST
F32, B16 = jnp.float32, jnp.bfloat16
VMEM = pltpu.VMEM


def spread(n_ka, b_ref, c_ref, out_ref):
    rows, rank = b_ref.shape
    b = jnp.concatenate([b_ref[: rows // 2], b_ref[rows // 2 :]], axis=1)
    c = jnp.concatenate([c_ref[...], jnp.zeros((8 - c_ref.shape[0], rank), F32)], axis=0)
    c = jnp.concatenate([c, c], axis=1)
    for peer in range(n_ka):
        out_ref[peer, : rows // 2] = b
        out_ref[peer, rows // 2 :] = c


def split(x):
    high = x.astype(B16)
    return high, (x - high.astype(F32)).astype(B16)


def transposed_dot(x, y):
    return lax.dot_general(x, y, (((0,), (0,)), ((), ())), precision=HI, preferred_element_type=F32)


def pack(n_ja, n_ka, t_ref, block_ref, c_ref, out_ref, gram_ref, sums_ref):
    ka = lax.axis_index("ka")
    peers = n_ja * n_ka
    depth, rows, cols = t_ref.shape
    rank = c_ref.shape[1]
    half = rank // 2
    b = jnp.concatenate([block_ref[:, :-8, :rank], block_ref[:, :-8, rank:]], axis=1).reshape(-1, rank)
    c_wide = block_ref[:, -8:].reshape(-1, 2 * rank)
    c_all = c_wide[:, :rank]
    wide = jnp.concatenate([b, b], axis=1)
    gram_ref[...] = transposed_dot(b, wide) * transposed_dot(c_all, c_wide)
    weights = []
    for k in range(depth):
        high, low = split(b * c_ref[k : k + 1, :])
        weights.append((high, jnp.concatenate([high, low], axis=1)))
    per = rows // peers
    step = rows // 4
    for at in range(0, rows, step):
        first = jnp.zeros((step, 2 * rank), F32)
        second = jnp.zeros((step, rank), F32)
        for k in range(depth):
            high, low = split(t_ref[k, at : at + step, :])
            first += jnp.dot(high, weights[k][1], preferred_element_type=F32)
            second += jnp.dot(low, weights[k][0], preferred_element_type=F32)
        sums_ref[at : at + step, :rank] = first[:, :rank] + (first[:, rank:] + second)
    lane = lax.broadcasted_iota(jnp.int32, (peers, 2 * rank), 1)
    for q in range(per):
        row = gram_ref[pl.ds(ka + 8 * q, 1), :]
        out_ref[pl.ds(q, peers, stride=5), :] = jnp.where(
            lane < rank, sums_ref[pl.ds(q, peers, stride=per), :], row
        )
    last = jnp.zeros((1, 2 * rank), F32)
    one = lax.broadcasted_iota(jnp.int32, (1, 2 * rank), 1)
    for q in range(4):
        row = gram_ref[pl.ds(half + ka + 8 * q, 1), :]
        row = pltpu.roll(row, (half * q - half) % (2 * rank), 1)
        last = jnp.where(one // half == q, row, last)
    out_ref[pl.ds(4, peers, stride=5), :] = jnp.broadcast_to(last, (peers, 2 * rank))


def inverse(x):
    r = pl.reciprocal(x, approx=True)
    r = r * (2.0 - x * r)
    return r * (2.0 - x * r)


def solve(n_ja, n_ka, got_ref, out_ref, sum_ref):
    rank = 64
    half = rank // 2
    wide = 2 * rank
    per = n_ka * 5
    parts = [got_ref[pl.ds(a * per, per), :] for a in range(n_ja)]
    while len(parts) > 1:
        parts = [x + y for x, y in zip(parts[::2], parts[1::2])]
    sum_ref[...] = parts[0]
    x = [sum_ref[pl.ds(q, n_ka, stride=5), :] for q in range(5)]
    lane = lax.broadcasted_iota(jnp.int32, (8, wide), 1)
    sub = lax.broadcasted_iota(jnp.int32, (8, wide), 0)
    upper = jnp.concatenate(x[:4], axis=0)
    flipped = jnp.transpose(upper)[rank + half :, :]
    groups = []
    for g in range(8):
        eye = jnp.where(lane == 8 * g + sub, 1.0, 0.0)
        if g < 4:
            right = x[g]
        else:
            corner = pltpu.roll(x[4], (96 - half * (g - 4)) % wide, 1)
            lower = flipped[8 * (g - 4) : 8 * (g - 3), :]
            lower = jnp.concatenate([lower] * 4, axis=1)
            right = jnp.where(lane < rank + half, lower, corner)
        groups.append(jnp.where(lane < rank, eye, right))
    sums = [jnp.sum(x[q], axis=0, keepdims=True) for q in range(4)]
    m = jnp.concatenate(sums + [jnp.zeros((4, wide), F32)], axis=0)
    m = pltpu.roll(m, rank, 1)
    groups.append(jnp.where(lane < rank, 0.0, m))

    def column(a, c):
        return jnp.broadcast_to(a[:, c : c + 1], (8, wide))

    def row(a, r):
        return jnp.broadcast_to(a[r : r + 1, :], (8, wide))

    for r in range(8):
        at = rank + 8 * r
        own = groups[r]
        cols = [column(own, at + s) for s in range(8)]
        pivots = {(u, v): row(cols[v], u) for u in range(8) for v in range(u + 1)}
        rows = [row(own, s) for s in range(8)]
        left = {g: [column(groups[g], at + s) for s in range(8)] for g in range(r + 1, 9)}
        for t in range(8):
            inv = inverse(pivots[t, t])
            scaled = rows[t] * inv
            ratio = {u: pivots[u, t] * inv for u in range(t + 1, 8)}
            for u in range(t + 1, 8):
                for v in range(t + 1, u + 1):
                    pivots[u, v] = pivots[u, v] - ratio[u] * pivots[v, t]
            for u in range(t + 1, 8):
                rows[u] = rows[u] - ratio[u] * rows[t]
            for g in range(r + 1, 9):
                groups[g] = groups[g] - left[g][t] * scaled
                for u in range(t + 1, 8):
                    left[g][u] = left[g][u] - ratio[u] * left[g][t]
    out_ref[...] = -groups[8][: out_ref.shape[0], :rank]


def per_device(tensor, factor_b, factor_c):
    n_ja, n_ka = lax.axis_size("ja"), lax.axis_size("ka")
    peers = n_ja * n_ka
    rows_b, rank = factor_b.shape
    mine = pl.pallas_call(
        functools.partial(spread, n_ka),
        out_shape=jax.ShapeDtypeStruct((n_ka, rows_b // 2 + 8, 2 * rank), F32),
        name="spread",
    )(factor_b, factor_c)
    block = lax.all_to_all(mine, "ka", 0, 0, tiled=True)
    packed = pl.pallas_call(
        functools.partial(pack, n_ja, n_ka),
        out_shape=jax.ShapeDtypeStruct((peers * 5, 2 * rank), F32),
        scratch_shapes=[
            pltpu.VMEM((rank, 2 * rank), F32),
            pltpu.VMEM((tensor.shape[1], 2 * rank), F32),
        ],
        compiler_params=pltpu.CompilerParams(vmem_limit_bytes=32 * 2**20),
        name="pack",
    )(tensor, block, factor_c)
    got = lax.all_to_all(packed.reshape(peers, 1, 10 * rank), ("ja", "ka"), 0, 0, tiled=True)
    return pl.pallas_call(
        functools.partial(solve, n_ja, n_ka),
        out_shape=jax.ShapeDtypeStruct((tensor.shape[1] // peers, rank), F32),
        scratch_shapes=[pltpu.VMEM((n_ka * 5, 2 * rank), F32)],
        compiler_params=pltpu.CompilerParams(vmem_limit_bytes=32 * 2**20),
        name="solve",
    )(got.reshape(peers * 5, 2 * rank))


def solution(mesh):
    in_specs = (P("ka", "ia", "ja"), P(("ja", "ka"), None), P("ka", None))
    out_specs = P(("ia", "ja", "ka"), None)
    return jax.shard_map(
        per_device, mesh=mesh, in_specs=in_specs, out_specs=out_specs, check_vma=False
    )
```

time: 60.7 us -> 47.1 us (0.78)
  other arithmetic: 13.9 us -> 0 us
  blocking collectives: 24.9 us -> 38.7 us
  starting transfers between devices: 10.1 us -> 0 us
  Pallas kernels: 0 us -> 5.76 us
  waiting for transfers between devices: 4.9 us -> 0 us
  matrix products: 4.21 us -> 0 us
    all_to_all x1 -> x2, blocking collectives: 24.9 us -> 38.7 us  [the longest x1 23.6 us: per_device(): lax.all_to_all(packed.reshape(peers, 1, 10 * rank), ('ja', 'ka'), 0, 0, t...]
    another operation x5 -> x0, other arithmetic: 12.1 us -> none  [the longest x3 6.52 us: per_device(): lower = jnp.linalg.cholesky(gram)]
    all_to_all x1 -> x0, starting transfers between devices: 10.1 us -> none  [per_device(): lax.all_to_all(jnp.broadcast_to(mine[None], (n_ka,) + mine.shape), 'ka',...]
    pallas_call x0 -> x3, Pallas kernels: none -> 5.76 us  [the longest x1 3.21 us: per_device(): pl.pallas_call(functools.partial(solve, n_ja, n_ka), out_shape=jax.ShapeD...]
    all_to_all x1 -> x0, waiting for transfers between devices: 4.9 us -> none  [per_device(): lax.all_to_all(jnp.broadcast_to(mine[None], (n_ka,) + mine.shape), 'ka',...]
    dot_general x3 -> x0, matrix products: 3.29 us -> none  [the longest x1 2.68 us: per_device(): partial_value = jnp.einsum('kij,jr->kir', tensor, b_block, precision=HI)]
    unnamed x5 -> x4, local copies, waits for them, and re-layouts: 0.87 us -> 2.27 us
    concatenate x2 -> x0, other arithmetic: 0.92 us -> none  [the longest x1 0.89 us: per_device(): mine = jnp.concatenate([factor_b, factor_c], axis=0)]
  transfers between devices with their start and end apart: 1 -> 0, of which waited for: 1 -> 0; matrix products, arithmetic and copies ran while one was open for 0% -> 0% of each run, Pallas kernels for 0% -> 0%
where the time goes in v2:
time: 47.1 us; the launch traced here: 46.7 us
  blocking collectives  38.7 us (82%)
  Pallas kernels  5.76 us (12%)
  local copies, waits for them, and re-layouts  2.27 us (5%)
    all_to_all x1, blocking collectives, per_device(): lax.all_to_all(packed.reshape(peers, 1, 10 * rank), ('ja', 'ka'), 0, 0, t...  23.6 us
    all_to_all x1, blocking collectives, per_device(): block = lax.all_to_all(mine, 'ka', 0, 0, tiled=True)  15.1 us
    pallas_call x1, Pallas kernels, per_device(): pl.pallas_call(functools.partial(solve, n_ja, n_ka), out_shape=jax.ShapeD...  3.21 us
    unnamed x4, local copies, waits for them, and re-layouts  2.27 us
    pallas_call x1, Pallas kernels, per_device(): pl.pallas_call(functools.partial(spread, n_ka), out_shape=jax.ShapeDtypeS...  1.42 us
    pallas_call x1, Pallas kernels, per_device(): pl.pallas_call(functools.partial(pack, n_ja, n_ka), out_shape=jax.ShapeDt...  1.13 us

profile of v2, /device:TPU:1, one launch (start us, length us, event | category | flops | bytes accessed | tf_op | source)
XLA Modules:
  0.0 46.7 jit_solution(1963540854241048488)
XLA Ops:
  0.0 1.4 %spread.1 = f32[8,24,128]{2,1,0:T(8,128)} custom-call(f32[32,64]{1,0:T(8,128)} %b_ref.1, f32[4,64]{1,0:T(4,128)} %c_ref.3), custom_call_target="tpu_custom_call" | custom-call | tf_op jit(solution)/shard_map/spread/pallas_call | solution.py:143
  1.4 15.1 %all_to_all.10.block_ref = f32[8,24,128]{2,1,0:T(8,128)S(1)} all-to-all(f32[8,24,128]{2,1,0:T(8,128)} %spread.1), channel_id=1, replica_groups=mesh['ia'=4,'ja'=16,'ka'=8] {'ka'}, dimensions={0} | all-to-all | bytes 196608 | tf_op jit(solution)/shard_map/all_to_all | solution.py:148
  16.5 0.0 copy-start
  16.5 1.6 %copy-done = f32[4,512,256]{2,1,0:T(8,128)S(1)} copy-done((f32[4,512,256]{2,1,0:T(8,128)S(1)}, f32[4,512,256]{2,1,0:T(8,128)}, u32[]{:S(2)}) %copy-start) | copy-done | bytes 2097176
  18.1 0.0 copy-start.1
  18.1 0.7 %copy-done.1 = f32[4,64]{1,0:T(4,128)S(1)} copy-done((f32[4,64]{1,0:T(4,128)S(1)}, f32[4,64]{1,0:T(4,128)}, u32[]{:S(2)}) %copy-start.1) | copy-done | bytes 1048
  18.8 1.1 %pack.1 = f32[640,128]{1,0:T(8,128)S(1)} custom-call(f32[4,512,256]{2,1,0:T(8,128)S(1)} %copy-done, f32[8,24,128]{2,1,0:T(8,128)S(1)} %all_to_all.10.block_ref, f32[4,64]{1,0:T(4,128)S(1)} %copy-done.1), custom_call_target="tpu_custom_call" | custom-call | tf_op jit(solution)/shard_map/pack/pallas_call | solution.py:149
  20.0 23.6 %all_to_all.11 = f32[128,1,640]{2,1,0:T(1,128)S(1)} all-to-all(f32[128,1,640]{2,1,0:T(1,128)S(1)} %bitcast.3), channel_id=1, replica_groups=mesh['ia'=4,'ja'=16,'ka'=8] {'ja','ka'}, dimensions={0} | all-to-all | bytes 655360 | tf_op jit(solution)/shard_map/all_to_all | solution.py:159
  43.5 3.2 %solve.1 = f32[4,64]{1,0:T(4,128)} custom-call(f32[640,128]{1,0:T(8,128)S(1)} %bitcast.2), custom_call_target="tpu_custom_call" | custom-call | tf_op jit(solution)/shard_map/solve/pallas_call | solution.py:160
Async XLA Ops:
  16.5 1.6 %copy-start = (f32[4,512,256]{2,1,0:T(8,128)S(1)}, f32[4,512,256]{2,1,0:T(8,128)}, u32[]{:S(2)}) copy-start(f32[4,512,256]{2,1,0:T(8,128)} %t_ref.1) | copy-start | bytes 6291460
  18.1 0.7 %copy-start.1 = (f32[4,64]{1,0:T(4,128)S(1)}, f32[4,64]{1,0:T(4,128)}, u32[]{:S(2)}) copy-start(f32[4,64]{1,0:T(4,128)} %c_ref.3) | copy-start | bytes 3076

commit v3 on v2

v3 whole, which is shorter than its diff:
```python
import functools

import jax
import jax.numpy as jnp
from jax import lax
from jax.experimental import pallas as pl
from jax.experimental.pallas import tpu as pltpu
from jax.sharding import Mesh
from jax.sharding import PartitionSpec as P

HI = lax.Precision.HIGHEST
F32, B16 = jnp.float32, jnp.bfloat16
BIG = pltpu.CompilerParams(vmem_limit_bytes=32 * 2**20)


def spread(n_ka, b_ref, c_ref, out_ref):
    rows, rank = b_ref.shape
    b = jnp.concatenate([b_ref[: rows // 2], b_ref[rows // 2 :]], axis=1)
    c = jnp.concatenate([c_ref[...], jnp.zeros((8 - c_ref.shape[0], rank), F32)], axis=0)
    c = jnp.concatenate([c, c], axis=1)
    for peer in range(n_ka):
        out_ref[peer, : rows // 2] = b
        out_ref[peer, rows // 2 :] = c


def split(x):
    high = x.astype(B16)
    return high, (x - high.astype(F32)).astype(B16)


def halve(t_ref, high_ref, low_ref):
    for k in range(t_ref.shape[0]):
        high_ref[k], low_ref[k] = split(t_ref[k])


def transposed_dot(x, y):
    return lax.dot_general(x, y, (((0,), (0,)), ((), ())), precision=HI, preferred_element_type=F32)


def contract(high_ref, low_ref, block_ref, sums_ref, piece_ref, gram_ref):
    x = lax.axis_index("x")
    ka = x * lax.axis_size("c") + lax.axis_index("c")
    depth, rows, cols = high_ref.shape
    rank = block_ref.shape[2] // 2
    wide = 2 * rank
    b = jnp.concatenate([block_ref[:, :-8, :rank], block_ref[:, :-8, rank:]], axis=1).reshape(-1, rank)
    c_wide = block_ref[:, -8:].reshape(-1, wide)
    gram_ref[...] = transposed_dot(b, jnp.concatenate([b, b], axis=1)) * transposed_dot(c_wide[:, :rank], c_wide)
    nothing = jnp.zeros(b.shape, B16)
    weights = []
    for k in range(depth):
        high, low = split(b * block_ref[ka, pl.ds(block_ref.shape[1] - 8 + k, 1), :rank])
        weights.append(
            (
                jnp.concatenate([high, low], axis=1),
                jnp.concatenate([high, nothing], axis=1),
                jnp.concatenate([low, high], axis=1),
                jnp.concatenate([nothing, high], axis=1),
            )
        )
    step = rows // 4
    lane = lax.broadcasted_iota(jnp.int32, (step, wide), 1)
    for at in range(0, rows // 2, step):
        sides = []
        for side in range(2):
            start = at + side * (rows // 2)
            first = jnp.zeros((step, wide), F32)
            second = jnp.zeros((step, wide), F32)
            for k in range(depth):
                first += jnp.dot(high_ref[k, start : start + step, :], weights[k][2 * side], preferred_element_type=F32)
                second += jnp.dot(low_ref[k, start : start + step, :], weights[k][2 * side + 1], preferred_element_type=F32)
            sides.append(first + (pltpu.roll(first, rank, 1) + second))
        sums_ref[at : at + step, :] = jnp.where(lane < rank, sides[0], sides[1])
    half = rank // 2
    lane = lax.broadcasted_iota(jnp.int32, (8, wide), 1)
    top = gram_ref[pl.ds(pl.multiple_of(8 * x, 8), 8), :]
    low = gram_ref[pl.ds(pl.multiple_of(half + 8 * x, 8), 8), :]
    moved = pltpu.roll(pltpu.roll(low, wide - half, 1), 4, 0)
    piece_ref[...] = jnp.where(lane < rank, jnp.where(lane < half, moved, low), top)


def compose(both_ref, piece_ref, out_ref):
    c = lax.axis_index("c")
    peers = out_ref.shape[0]
    wide = out_ref.shape[2]
    lane = lax.broadcasted_iota(jnp.int32, (8, wide), 1)
    sub = lax.broadcasted_iota(jnp.int32, (8, wide), 0)
    own = (sub < 4) & (lane < wide // 2)
    piece = piece_ref[...]
    for p in range(peers // 2):
        rows = both_ref[0, 8 * p : 8 * p + 8, :] + both_ref[1, 8 * p : 8 * p + 8, :]
        rows = jnp.where(c == 0, rows, pltpu.roll(rows, 4, 0))
        out_ref[p] = jnp.where(own, rows, piece)
        out_ref[p + peers // 2] = jnp.where(own, pltpu.roll(rows, wide // 2, 1), piece)


def inverse(x):
    r = pl.reciprocal(x, approx=True)
    r = r * (2.0 - x * r)
    return r * (2.0 - x * r)


def total(parts):
    while len(parts) > 1:
        parts = [x + y for x, y in zip(parts[::2], parts[1::2])]
    return parts[0]


def solve(n_x, got_ref, out_ref):
    wide = got_ref.shape[2]
    rank = wide // 2
    half = rank // 2
    n_ja = got_ref.shape[0] // n_x
    x = [total([got_ref[a * n_x + s] for a in range(n_ja)]) for s in range(n_x)]
    lane = lax.broadcasted_iota(jnp.int32, (8, wide), 1)
    sub = lax.broadcasted_iota(jnp.int32, (8, wide), 0)
    flipped = jnp.transpose(jnp.concatenate(x, axis=0))[rank + half :, :]
    groups = []
    for g in range(8):
        if g < 4:
            right = x[g]
        else:
            near = x[g - 4]
            corner = jnp.where(sub < 4, pltpu.roll(pltpu.roll(near, 4, 0), rank + half, 1), pltpu.roll(near, rank, 1))
            left = jnp.concatenate([flipped[8 * (g - 4) : 8 * (g - 3), :]] * 4, axis=1)
            right = jnp.where(lane < rank + half, left, corner)
        groups.append(jnp.where(lane < rank, jnp.where(lane == 8 * g + sub, 1.0, 0.0), right))
    m = pltpu.roll(total(x), rank, 1)
    groups.append(jnp.where((lane >= rank) & (sub < 4), m, 0.0))

    def column(a, c):
        return jnp.broadcast_to(a[:, c : c + 1], (8, wide))

    def row(a, r):
        return jnp.broadcast_to(a[r : r + 1, :], (8, wide))

    for r in range(8):
        at = rank + 8 * r
        own = groups[r]
        cols = [column(own, at + s) for s in range(8)]
        pivots = {(u, v): row(cols[v], u) for u in range(8) for v in range(u + 1)}
        rows = [row(own, s) for s in range(8)]
        left = {g: [column(groups[g], at + s) for s in range(8)] for g in range(r + 1, 9)}
        for t in range(8):
            inv = inverse(pivots[t, t])
            scaled = rows[t] * inv
            ratio = {u: pivots[u, t] * inv for u in range(t + 1, 8)}
            for u in range(t + 1, 8):
                for v in range(t + 1, u + 1):
                    pivots[u, v] = pivots[u, v] - ratio[u] * pivots[v, t]
            for u in range(t + 1, 8):
                rows[u] = rows[u] - ratio[u] * rows[t]
            for g in range(r + 1, 9):
                groups[g] = groups[g] - left[g][t] * scaled
                for u in range(t + 1, 8):
                    left[g][u] = left[g][u] - ratio[u] * left[g][t]
    out_ref[...] = -groups[8][: out_ref.shape[0], :rank]


def array(*shape, dtype=F32):
    return jax.ShapeDtypeStruct(shape, dtype)


def per_device(tensor, factor_b, factor_c):
    n_ja, n_x, n_c = lax.axis_size("ja"), lax.axis_size("x"), lax.axis_size("c")
    n_ka = n_x * n_c
    rows_b, rank = factor_b.shape
    rows = tensor.shape[1]
    mine = pl.pallas_call(
        functools.partial(spread, n_ka), out_shape=array(n_ka, rows_b // 2 + 8, 2 * rank), name="spread"
    )(factor_b, factor_c)
    high, low = pl.pallas_call(
        halve,
        out_shape=[array(*tensor.shape, dtype=B16)] * 2,
        compiler_params=BIG,
        cost_estimate=pl.CostEstimate(flops=2**21, bytes_accessed=2**22, transcendentals=0),
        name="halve",
    )(tensor)
    block = lax.all_to_all(mine, ("x", "c"), 0, 0, tiled=True)
    sums, piece = pl.pallas_call(
        contract,
        out_shape=[array(rows // 2, 2 * rank), array(8, 2 * rank)],
        scratch_shapes=[pltpu.VMEM((rank, 2 * rank), F32)],
        compiler_params=BIG,
        name="contract",
    )(high, low, block)
    both = lax.all_gather(sums, "c")
    packed = pl.pallas_call(
        compose, out_shape=array(n_ja * n_x, 8, 2 * rank), compiler_params=BIG, name="compose"
    )(both, piece)
    got = lax.all_to_all(packed, ("ja", "x"), 0, 0, tiled=True)
    return pl.pallas_call(
        functools.partial(solve, n_x), out_shape=array(rows // (n_ja * n_ka), rank), compiler_params=BIG, name="solve"
    )(got)


def solution(mesh):
    n = mesh.shape
    mesh = Mesh(mesh.devices.reshape(n["ia"], n["ja"], n["ka"] // 2, 2), ("ia", "ja", "x", "c"))
    ka = ("x", "c")
    in_specs = (P(ka, "ia", "ja"), P(("ja", *ka), None), P(ka, None))
    out_specs = P(("ia", "ja", *ka), None)
    return jax.shard_map(
        per_device, mesh=mesh, in_specs=in_specs, out_specs=out_specs, check_vma=False
    )
```

time: 47.1 us -> 42.1 us (0.89)
  the two profiles are of different devices: /device:TPU:1 before, /device:TPU:128 now
where the time goes in v3:
time: 42.1 us; the launch traced here: 41.8 us
  blocking collectives  25.9 us (62%)
  Pallas kernels  6.13 us (15%)
  starting transfers between devices  4.3 us (10%)
  waiting for transfers between devices  3.83 us (9%)
  local copies, waits for them, and re-layouts  1.59 us (4%)
    all_to_all x1, blocking collectives, per_device(): got = lax.all_to_all(packed, ('ja', 'x'), 0, 0, tiled=True)  23.9 us
    all_to_all x1, starting transfers between devices, per_device(): block = lax.all_to_all(mine, ('x', 'c'), 0, 0, tiled=True)  4.3 us
    all_to_all x1, waiting for transfers between devices, per_device(): block = lax.all_to_all(mine, ('x', 'c'), 0, 0, tiled=True)  3.83 us
    pallas_call x1, Pallas kernels, per_device(): pl.pallas_call(functools.partial(solve, n_x), out_shape=array(rows // (n_...  3.21 us
    all_gather x1, blocking collectives, per_device(): both = lax.all_gather(sums, 'c')  1.99 us
    unnamed x2, local copies, waits for them, and re-layouts  1.59 us
    pallas_call x1, Pallas kernels, per_device(): pl.pallas_call(functools.partial(spread, n_ka), out_shape=array(n_ka, row...  1.43 us
    pallas_call x1, Pallas kernels, per_device(): pl.pallas_call(contract, out_shape=[array(rows // 2, 2 * rank), array(8,...  1.01 us
  transfers between devices with their start and end apart: 1, of which 1 were waited for; matrix products, arithmetic and copies ran while one was open for 0% of the time, Pallas kernels for 1%

profile of v3, /device:TPU:128, one launch (start us, length us, event | category | flops | bytes accessed | tf_op | source)
XLA Modules:
  0.0 41.8 jit_solution(1141115566661953411)
XLA Ops:
  0.0 1.4 %spread.1 = f32[8,24,128]{2,1,0:T(8,128)} custom-call(f32[32,64]{1,0:T(8,128)} %b_ref.1, f32[4,64]{1,0:T(4,128)} %c_ref.1), custom_call_target="tpu_custom_call" | custom-call | tf_op jit(solution)/shard_map/spread/pallas_call | solution.py:169
  1.4 4.3 %all-to-all-start = ((f32[8,24,128]{2,1,0:T(8,128)}), f32[8,24,128]{2,1,0:T(8,128)S(1)}, u32[]{:S(2)}, u32[]{:S(2)}) async-start(f32[8,24,128]{2,1,0:T(8,128)} %spread.1), calls=%async_computation | async-start | bytes 196608 | tf_op jit(solution)/shard_map/all_to_all | solution.py:179
  5.7 0.0 copy-start
  5.7 1.6 %copy-done = f32[4,512,256]{2,1,0:T(8,128)S(1)} copy-done((f32[4,512,256]{2,1,0:T(8,128)S(1)}, f32[4,512,256]{2,1,0:T(8,128)}, u32[]{:S(2)}) %copy-start) | copy-done | bytes 2097176
  7.3 0.4 halve.1
  7.7 3.8 %all-to-all-done.block_ref = f32[8,24,128]{2,1,0:T(8,128)S(1)} async-done(((f32[8,24,128]{2,1,0:T(8,128)}), f32[8,24,128]{2,1,0:T(8,128)S(1)}, u32[]{:S(2)}, u32[]{:S(2)}) %all-to-all-start) | async-done | bytes 98336 | tf_op jit(solution)/shard_map/all_to_all | solution.py:179
  11.5 1.0 %contract.1 = (f32[256,128]{1,0:T(8,128)S(1)}, f32[8,128]{1,0:T(8,128)S(1)}) custom-call(bf16[4,512,256]{2,1,0:T(8,128)(2,1)S(1)} %get-tuple-element.9.high_ref, bf16[4,512,256]{2,1,0:T(8,128)(2,1)S(1)} %get-tuple-element.10.low_ref, f32[8,24,128]{2,1,0:T(8,128)S(1)} %all-to-all-done.block_ref), custom_call_target="tpu_custom_call" | custom-call | tf_op jit(solution)/shard_map/contract/pallas_call | solution.py:180
  12.6 2.0 %all-gather = f32[512,128]{1,0:T(8,128)S(1)} all-gather(f32[256,128]{1,0:T(8,128)S(1)} %get-tuple-element.11), channel_id=2, replica_groups=mesh['ia'=4,'ja'=16,'x'=4,'c'=2] {'c'}, dimensions={0}, use_global_device_ids=true | all-gather | bytes 393216 | tf_op jit(solution)/shard_map/all_gather | solution.py:187
  14.5 0.1 compose.1
  14.7 23.9 %all_to_all.10.got_ref = f32[64,8,128]{2,1,0:T(8,128)S(1)} all-to-all(f32[64,8,128]{2,1,0:T(8,128)S(1)} %compose.1), channel_id=1, replica_groups=mesh['ia'=4,'ja'=16,'x'=4,'c'=2] {'ja','x'}, dimensions={0} | all-to-all | bytes 524288 | tf_op jit(solution)/shard_map/all_to_all | solution.py:191
  38.5 3.2 %solve.1 = f32[4,64]{1,0:T(4,128)} custom-call(f32[64,8,128]{2,1,0:T(8,128)S(1)} %all_to_all.10.got_ref), custom_call_target="tpu_custom_call" | custom-call | tf_op jit(solution)/shard_map/solve/pallas_call | solution.py:192
Async XLA Ops:
  1.4 10.1 %all-to-all-start = ((f32[8,24,128]{2,1,0:T(8,128)}), f32[8,24,128]{2,1,0:T(8,128)S(1)}, u32[]{:S(2)}, u32[]{:S(2)}) async-start(f32[8,24,128]{2,1,0:T(8,128)} %spread.1), calls=%async_computation | async-start | bytes 196608 | tf_op jit(solution)/shard_map/all_to_all | solution.py:179
  5.7 1.6 %copy-start = (f32[4,512,256]{2,1,0:T(8,128)S(1)}, f32[4,512,256]{2,1,0:T(8,128)}, u32[]{:S(2)}) copy-start(f32[4,512,256]{2,1,0:T(8,128)} %t_ref.1) | copy-start | bytes 6291460

commit v4 on v3

--- a/solution.py
+++ b/solution.py
@@ -13,10 +13,15 @@
 BIG = pltpu.CompilerParams(vmem_limit_bytes=32 * 2**20)
 
 
-def spread(n_ka, b_ref, c_ref, out_ref):
-    rows, rank = b_ref.shape
-    b = jnp.concatenate([b_ref[: rows // 2], b_ref[rows // 2 :]], axis=1)
-    c = jnp.concatenate([c_ref[...], jnp.zeros((8 - c_ref.shape[0], rank), F32)], axis=0)
+def spread(n_ka, b_ref, c_ref, out_ref, b_own, c_own, sems):
+    copies = [pltpu.make_async_copy(b_ref, b_own, sems.at[0]), pltpu.make_async_copy(c_ref, c_own, sems.at[1])]
+    for copy in copies:
+        copy.start()
+    for copy in copies:
+        copy.wait()
+    rows, rank = b_own.shape
+    b = jnp.concatenate([b_own[: rows // 2], b_own[rows // 2 :]], axis=1)
+    c = jnp.concatenate([c_own[...], jnp.zeros((8 - c_own.shape[0], rank), F32)], axis=0)
     c = jnp.concatenate([c, c], axis=1)
     for peer in range(n_ka):
         out_ref[peer, : rows // 2] = b
@@ -94,12 +99,6 @@
         out_ref[p + peers // 2] = jnp.where(own, pltpu.roll(rows, wide // 2, 1), piece)
 
 
-def inverse(x):
-    r = pl.reciprocal(x, approx=True)
-    r = r * (2.0 - x * r)
-    return r * (2.0 - x * r)
-
-
 def total(parts):
     while len(parts) > 1:
         parts = [x + y for x, y in zip(parts[::2], parts[1::2])]
@@ -129,31 +128,33 @@
     groups.append(jnp.where((lane >= rank) & (sub < 4), m, 0.0))
 
     def column(a, c):
-        return jnp.broadcast_to(a[:, c : c + 1], (8, wide))
+        return jnp.take_along_axis(a, jnp.full((8, wide), c, jnp.int32), axis=1)
 
     def row(a, r):
-        return jnp.broadcast_to(a[r : r + 1, :], (8, wide))
+        return jnp.take_along_axis(a, jnp.full((8, wide), r, jnp.int32), axis=0)
 
     for r in range(8):
         at = rank + 8 * r
-        own = groups[r]
-        cols = [column(own, at + s) for s in range(8)]
-        pivots = {(u, v): row(cols[v], u) for u in range(8) for v in range(u + 1)}
-        rows = [row(own, s) for s in range(8)]
-        left = {g: [column(groups[g], at + s) for s in range(8)] for g in range(r + 1, 9)}
+        later = range(r + 1, 9)
+        rows = [row(groups[r], s) for s in range(8)]
+        pivots = {(u, v): column(rows[u], at + v) for u in range(8) for v in range(u + 1)}
+        left = {g: [column(groups[g], at + s) for s in range(8)] for g in later}
+        terms = {g: [] for g in later}
         for t in range(8):
-            inv = inverse(pivots[t, t])
+            inv = 1.0 / pivots[t, t]
             scaled = rows[t] * inv
             ratio = {u: pivots[u, t] * inv for u in range(t + 1, 8)}
             for u in range(t + 1, 8):
                 for v in range(t + 1, u + 1):
                     pivots[u, v] = pivots[u, v] - ratio[u] * pivots[v, t]
-            for u in range(t + 1, 8):
                 rows[u] = rows[u] - ratio[u] * rows[t]
-            for g in range(r + 1, 9):
-                groups[g] = groups[g] - left[g][t] * scaled
+            for g in later:
+                terms[g].append(left[g][t] * scaled)
                 for u in range(t + 1, 8):
                     left[g][u] = left[g][u] - ratio[u] * left[g][t]
+        for g in later:
+            head, tail = terms[g][:4], terms[g][4:]
+            groups[g] = groups[g] - (total(head) + (total(tail[:2]) + tail[2]) + tail[3])
     out_ref[...] = -groups[8][: out_ref.shape[0], :rank]
 
 
@@ -167,7 +168,15 @@
     rows_b, rank = factor_b.shape
     rows = tensor.shape[1]
     mine = pl.pallas_call(
-        functools.partial(spread, n_ka), out_shape=array(n_ka, rows_b // 2 + 8, 2 * rank), name="spread"
+        functools.partial(spread, n_ka),
+        out_shape=array(n_ka, rows_b // 2 + 8, 2 * rank),
+        in_specs=[pl.BlockSpec(memory_space=pl.ANY)] * 2,
+        scratch_shapes=[
+            pltpu.VMEM(factor_b.shape, F32),
+            pltpu.VMEM(factor_c.shape, F32),
+            pltpu.SemaphoreType.DMA((2,)),
+        ],
+        name="spread",
     )(factor_b, factor_c)
     high, low = pl.pallas_call(
         halve,

time: 42.1 us -> 41 us (0.974)
  Pallas kernels: 6.13 us -> 4.96 us
    pallas_call x1, Pallas kernels: 3.21 us -> 2.02 us  [per_device(): pl.pallas_call(functools.partial(solve, n_x), out_shape=array(rows // (n_...]
where the time goes in v4:
time: 41 us; the launch traced here: 40.6 us
  blocking collectives  25.9 us (63%)
  Pallas kernels  4.96 us (12%)
  starting transfers between devices  4.31 us (11%)
  waiting for transfers between devices  3.83 us (9%)
  local copies, waits for them, and re-layouts  1.59 us (4%)
    all_to_all x1, blocking collectives, per_device(): got = lax.all_to_all(packed, ('ja', 'x'), 0, 0, tiled=True)  23.9 us
    all_to_all x1, starting transfers between devices, per_device(): block = lax.all_to_all(mine, ('x', 'c'), 0, 0, tiled=True)  4.31 us
    all_to_all x1, waiting for transfers between devices, per_device(): block = lax.all_to_all(mine, ('x', 'c'), 0, 0, tiled=True)  3.83 us
    pallas_call x1, Pallas kernels, per_device(): pl.pallas_call(functools.partial(solve, n_x), out_shape=array(rows // (n_...  2.02 us
    all_gather x1, blocking collectives, per_device(): both = lax.all_gather(sums, 'c')  1.99 us
    unnamed x2, local copies, waits for them, and re-layouts  1.59 us
    pallas_call x1, Pallas kernels, per_device(): pl.pallas_call(functools.partial(spread, n_ka), out_shape=array(n_ka, row...  1.45 us
    pallas_call x1, Pallas kernels, per_device(): pl.pallas_call(contract, out_shape=[array(rows // 2, 2 * rank), array(8,...  1.01 us
  transfers between devices with their start and end apart: 1, of which 1 were waited for; matrix products, arithmetic and copies ran while one was open for 0% of the time, Pallas kernels for 1%

profile of v4, /device:TPU:128, one launch (start us, length us, event | category | flops | bytes accessed | tf_op | source)
XLA Modules:
  0.0 40.6 jit_solution(1021161014901880350)
XLA Ops:
  0.0 1.4 %spread.1 = f32[8,24,128]{2,1,0:T(8,128)} custom-call(f32[32,64]{1,0:T(8,128)} %b_ref.1, f32[4,64]{1,0:T(4,128)} %c_ref.1), custom_call_target="tpu_custom_call" | custom-call | tf_op jit(solution)/shard_map/spread/pallas_call | solution.py:170
  1.5 4.3 %all-to-all-start = ((f32[8,24,128]{2,1,0:T(8,128)}), f32[8,24,128]{2,1,0:T(8,128)S(1)}, u32[]{:S(2)}, u32[]{:S(2)}) async-start(f32[8,24,128]{2,1,0:T(8,128)} %spread.1), calls=%async_computation | async-start | bytes 196608 | tf_op jit(solution)/shard_map/all_to_all | solution.py:188
  5.8 0.0 copy-start
  5.8 1.6 %copy-done = f32[4,512,256]{2,1,0:T(8,128)S(1)} copy-done((f32[4,512,256]{2,1,0:T(8,128)S(1)}, f32[4,512,256]{2,1,0:T(8,128)}, u32[]{:S(2)}) %copy-start) | copy-done | bytes 2097176
  7.4 0.4 halve.1
  7.7 3.8 %all-to-all-done.block_ref = f32[8,24,128]{2,1,0:T(8,128)S(1)} async-done(((f32[8,24,128]{2,1,0:T(8,128)}), f32[8,24,128]{2,1,0:T(8,128)S(1)}, u32[]{:S(2)}, u32[]{:S(2)}) %all-to-all-start) | async-done | bytes 98336 | tf_op jit(solution)/shard_map/all_to_all | solution.py:188
  11.6 1.0 %contract.1 = (f32[256,128]{1,0:T(8,128)S(1)}, f32[8,128]{1,0:T(8,128)S(1)}) custom-call(bf16[4,512,256]{2,1,0:T(8,128)(2,1)S(1)} %get-tuple-element.9.high_ref, bf16[4,512,256]{2,1,0:T(8,128)(2,1)S(1)} %get-tuple-element.10.low_ref, f32[8,24,128]{2,1,0:T(8,128)S(1)} %all-to-all-done.block_ref), custom_call_target="tpu_custom_call" | custom-call | tf_op jit(solution)/shard_map/contract/pallas_call | solution.py:189
  12.6 2.0 %all-gather = f32[512,128]{1,0:T(8,128)S(1)} all-gather(f32[256,128]{1,0:T(8,128)S(1)} %get-tuple-element.11), channel_id=2, replica_groups=mesh['ia'=4,'ja'=16,'x'=4,'c'=2] {'c'}, dimensions={0}, use_global_device_ids=true | all-gather | bytes 393216 | tf_op jit(solution)/shard_map/all_gather | solution.py:196
  14.6 0.1 compose.1
  14.7 23.9 %all_to_all.10.got_ref = f32[64,8,128]{2,1,0:T(8,128)S(1)} all-to-all(f32[64,8,128]{2,1,0:T(8,128)S(1)} %compose.1), channel_id=1, replica_groups=mesh['ia'=4,'ja'=16,'x'=4,'c'=2] {'ja','x'}, dimensions={0} | all-to-all | bytes 524288 | tf_op jit(solution)/shard_map/all_to_all | solution.py:200
  38.6 2.0 %solve.1 = f32[4,64]{1,0:T(4,128)} custom-call(f32[64,8,128]{2,1,0:T(8,128)S(1)} %all_to_all.10.got_ref), custom_call_target="tpu_custom_call" | custom-call | tf_op jit(solution)/shard_map/solve/pallas_call | solution.py:201
Async XLA Ops:
  1.5 10.1 %all-to-all-start = ((f32[8,24,128]{2,1,0:T(8,128)}), f32[8,24,128]{2,1,0:T(8,128)S(1)}, u32[]{:S(2)}, u32[]{:S(2)}) async-start(f32[8,24,128]{2,1,0:T(8,128)} %spread.1), calls=%async_computation | async-start | bytes 196608 | tf_op jit(solution)/shard_map/all_to_all | solution.py:188
  5.8 1.6 %copy-start = (f32[4,512,256]{2,1,0:T(8,128)S(1)}, f32[4,512,256]{2,1,0:T(8,128)}, u32[]{:S(2)}) copy-start(f32[4,512,256]{2,1,0:T(8,128)} %t_ref.1) | copy-start | bytes 6291460

commit v5 on v4

--- a/solution.py
+++ b/solution.py
@@ -76,27 +76,36 @@
                 second += jnp.dot(low_ref[k, start : start + step, :], weights[k][2 * side + 1], preferred_element_type=F32)
             sides.append(first + (pltpu.roll(first, rank, 1) + second))
         sums_ref[at : at + step, :] = jnp.where(lane < rank, sides[0], sides[1])
-    half = rank // 2
-    lane = lax.broadcasted_iota(jnp.int32, (8, wide), 1)
-    top = gram_ref[pl.ds(pl.multiple_of(8 * x, 8), 8), :]
-    low = gram_ref[pl.ds(pl.multiple_of(half + 8 * x, 8), 8), :]
-    moved = pltpu.roll(pltpu.roll(low, wide - half, 1), 4, 0)
-    piece_ref[...] = jnp.where(lane < rank, jnp.where(lane < half, moved, low), top)
+    own = gram_ref[pl.ds(x, 16, stride=4), :]
+    by16, by80, by96 = (pltpu.roll(own, n, 1) for n in (16, 80, 96))
+    lane = lax.broadcasted_iota(jnp.int32, (1, wide), 1)
+
+    def one(a, m):
+        return a[m : m + 1, :]
+
+    for r in range(4):
+        piece_ref[r : r + 1, :] = one(own, r)
+    for r in range(4, 7):
+        left = jnp.where(lane < 16, one(by80, 15), one(own, 7))
+        if r > 4:
+            left = jnp.where(lane < 32, one(by96, 2 * r - 1), one(own, 2 * r - 2))
+        right = jnp.where(lane < rank + 16, one(by16, r + 8), one(own, r))
+        piece_ref[r : r + 1, :] = jnp.where(lane < rank, left, right)
+    piece_ref[7:8, :] = jnp.zeros((1, wide), F32)
 
 
 def compose(both_ref, piece_ref, out_ref):
     c = lax.axis_index("c")
-    peers = out_ref.shape[0]
-    wide = out_ref.shape[2]
-    lane = lax.broadcasted_iota(jnp.int32, (8, wide), 1)
-    sub = lax.broadcasted_iota(jnp.int32, (8, wide), 0)
-    own = (sub < 4) & (lane < wide // 2)
-    piece = piece_ref[...]
-    for p in range(peers // 2):
-        rows = both_ref[0, 8 * p : 8 * p + 8, :] + both_ref[1, 8 * p : 8 * p + 8, :]
-        rows = jnp.where(c == 0, rows, pltpu.roll(rows, 4, 0))
-        out_ref[p] = jnp.where(own, rows, piece)
-        out_ref[p + peers // 2] = jnp.where(own, pltpu.roll(rows, wide // 2, 1), piece)
+    wide = out_ref.shape[1]
+    half = both_ref.shape[1] // 8
+    lane = lax.broadcasted_iota(jnp.int32, (half, wide), 1)
+    for r in range(4):
+        rows = both_ref[0, pl.ds(4 * c + r, half, stride=8), :] + both_ref[1, pl.ds(4 * c + r, half, stride=8), :]
+        line = piece_ref[r : r + 1, :]
+        out_ref[pl.ds(r, half, stride=7), :] = jnp.where(lane < wide // 2, rows, line)
+        out_ref[pl.ds(7 * half + r, half, stride=7), :] = jnp.where(lane < wide // 2, pltpu.roll(rows, wide // 2, 1), line)
+    for r in range(4, 7):
+        out_ref[pl.ds(r, 2 * half, stride=7), :] = jnp.broadcast_to(piece_ref[r : r + 1, :], (2 * half, wide))
 
 
 def total(parts):
@@ -105,27 +114,28 @@
     return parts[0]
 
 
-def solve(n_x, got_ref, out_ref):
-    wide = got_ref.shape[2]
+def solve(n_x, got_ref, out_ref, sum_ref):
+    wide = got_ref.shape[1]
     rank = wide // 2
-    half = rank // 2
-    n_ja = got_ref.shape[0] // n_x
-    x = [total([got_ref[a * n_x + s] for a in range(n_ja)]) for s in range(n_x)]
+    two = 2 * 7 * n_x
+    sum_ref[...] = total([got_ref[at : at + two, :] for at in range(0, got_ref.shape[0], two)])
     lane = lax.broadcasted_iota(jnp.int32, (8, wide), 1)
     sub = lax.broadcasted_iota(jnp.int32, (8, wide), 0)
-    flipped = jnp.transpose(jnp.concatenate(x, axis=0))[rank + half :, :]
+    parts = [sum_ref[pl.ds(r, 8, stride=7), :] for r in range(7)]
+    z = [part + pltpu.roll(part, 4, 0) for part in parts]
+    by48 = [pltpu.roll(z[r], 48, 1) for r in (4, 5, 6)]
+    by64 = [pltpu.roll(z[r], 64, 1) for r in (4, 5, 6)]
+    by96 = [pltpu.roll(z[r], 96, 1) for r in (5, 6)]
+    pieces = z[:7] + [by64[0], by64[1], by96[0], by64[2], by96[1]] + by48 + [pltpu.roll(z[4], 112, 1)]
+    upper = [jnp.where(sub < 4, pieces[2 * g], pieces[2 * g + 1]) for g in range(8)]
+    flipped = jnp.transpose(jnp.concatenate(upper, axis=0))[rank:, :]
     groups = []
     for g in range(8):
-        if g < 4:
-            right = x[g]
-        else:
-            near = x[g - 4]
-            corner = jnp.where(sub < 4, pltpu.roll(pltpu.roll(near, 4, 0), rank + half, 1), pltpu.roll(near, rank, 1))
-            left = jnp.concatenate([flipped[8 * (g - 4) : 8 * (g - 3), :]] * 4, axis=1)
-            right = jnp.where(lane < rank + half, left, corner)
+        left = flipped[8 * g : 8 * g + 8, :]
+        right = jnp.where(lane < rank + 16 * (g // 2), jnp.concatenate([left, left], axis=1), upper[g]) if g > 1 else upper[g]
         groups.append(jnp.where(lane < rank, jnp.where(lane == 8 * g + sub, 1.0, 0.0), right))
-    m = pltpu.roll(total(x), rank, 1)
-    groups.append(jnp.where((lane >= rank) & (sub < 4), m, 0.0))
+    m = jnp.concatenate([jnp.sum(parts[r], axis=0, keepdims=True) for r in range(4)] + [jnp.zeros((4, wide), F32)], axis=0)
+    groups.append(jnp.where(lane >= rank, pltpu.roll(m, rank, 1), 0.0))
 
     def column(a, c):
         return jnp.take_along_axis(a, jnp.full((8, wide), c, jnp.int32), axis=1)
@@ -195,12 +205,16 @@
     )(high, low, block)
     both = lax.all_gather(sums, "c")
     packed = pl.pallas_call(
-        compose, out_shape=array(n_ja * n_x, 8, 2 * rank), compiler_params=BIG, name="compose"
+        compose, out_shape=array(n_ja * n_x * 7, 2 * rank), compiler_params=BIG, name="compose"
     )(both, piece)
-    got = lax.all_to_all(packed, ("ja", "x"), 0, 0, tiled=True)
+    got = lax.all_to_all(packed.reshape(n_ja * n_x, 1, 14 * rank), ("ja", "x"), 0, 0, tiled=True)
     return pl.pallas_call(
-        functools.partial(solve, n_x), out_shape=array(rows // (n_ja * n_ka), rank), compiler_params=BIG, name="solve"
-    )(got)
+        functools.partial(solve, n_x),
+        out_shape=array(rows // (n_ja * n_ka), rank),
+        scratch_shapes=[pltpu.VMEM((14 * n_x, 2 * rank), F32)],
+        compiler_params=BIG,
+        name="solve",
+    )(got.reshape(n_ja * n_x * 7, 2 * rank))
 
 
 def solution(mesh):

time: 41 us -> 40.4 us (0.985)
  blocking collectives: 25.9 us -> 25.3 us
    all_to_all x1, blocking collectives: 23.9 us -> 23.3 us  [per_device(): lax.all_to_all(packed.reshape(n_ja * n_x, 1, 14 * rank), ('ja', 'x'), 0,...]
where the time goes in v5:
time: 40.4 us; the launch traced here: 40.1 us
  blocking collectives  25.3 us (63%)
  Pallas kernels  5 us (12%)
  starting transfers between devices  4.31 us (11%)
  waiting for transfers between devices  3.83 us (9%)
  local copies, waits for them, and re-layouts  1.59 us (4%)
    all_to_all x1, blocking collectives, per_device(): lax.all_to_all(packed.reshape(n_ja * n_x, 1, 14 * rank), ('ja', 'x'), 0,...  23.3 us
    all_to_all x1, starting transfers between devices, per_device(): block = lax.all_to_all(mine, ('x', 'c'), 0, 0, tiled=True)  4.31 us
    all_to_all x1, waiting for transfers between devices, per_device(): block = lax.all_to_all(mine, ('x', 'c'), 0, 0, tiled=True)  3.83 us
    pallas_call x1, Pallas kernels, per_device(): pl.pallas_call(functools.partial(solve, n_x), out_shape=array(rows // (n_...  2.06 us
    all_gather x1, blocking collectives, per_device(): both = lax.all_gather(sums, 'c')  1.99 us
    unnamed x2, local copies, waits for them, and re-layouts  1.59 us
    pallas_call x1, Pallas kernels, per_device(): pl.pallas_call(functools.partial(spread, n_ka), out_shape=array(n_ka, row...  1.45 us
    pallas_call x1, Pallas kernels, per_device(): pl.pallas_call(contract, out_shape=[array(rows // 2, 2 * rank), array(8,...  1.01 us
  transfers between devices with their start and end apart: 1, of which 1 were waited for; matrix products, arithmetic and copies ran while one was open for 0% of the time, Pallas kernels for 1%

profile of v5, /device:TPU:128, one launch (start us, length us, event | category | flops | bytes accessed | tf_op | source)
XLA Modules:
  0.0 40.1 jit_solution(8946473671361220075)
XLA Ops:
  0.0 1.4 %spread.1 = f32[8,24,128]{2,1,0:T(8,128)} custom-call(f32[32,64]{1,0:T(8,128)} %b_ref.1, f32[4,64]{1,0:T(4,128)} %c_ref.1), custom_call_target="tpu_custom_call" | custom-call | tf_op jit(solution)/shard_map/spread/pallas_call | solution.py:180
  1.5 4.3 %all-to-all-start = ((f32[8,24,128]{2,1,0:T(8,128)}), f32[8,24,128]{2,1,0:T(8,128)S(1)}, u32[]{:S(2)}, u32[]{:S(2)}) async-start(f32[8,24,128]{2,1,0:T(8,128)} %spread.1), calls=%async_computation | async-start | bytes 196608 | tf_op jit(solution)/shard_map/all_to_all | solution.py:198
  5.8 0.0 copy-start
  5.8 1.6 %copy-done = f32[4,512,256]{2,1,0:T(8,128)S(1)} copy-done((f32[4,512,256]{2,1,0:T(8,128)S(1)}, f32[4,512,256]{2,1,0:T(8,128)}, u32[]{:S(2)}) %copy-start) | copy-done | bytes 2097176
  7.4 0.4 halve.1
  7.7 3.8 %all-to-all-done.block_ref = f32[8,24,128]{2,1,0:T(8,128)S(1)} async-done(((f32[8,24,128]{2,1,0:T(8,128)}), f32[8,24,128]{2,1,0:T(8,128)S(1)}, u32[]{:S(2)}, u32[]{:S(2)}) %all-to-all-start) | async-done | bytes 98336 | tf_op jit(solution)/shard_map/all_to_all | solution.py:198
  11.6 1.0 %contract.1 = (f32[256,128]{1,0:T(8,128)S(1)}, f32[8,128]{1,0:T(8,128)S(1)}) custom-call(bf16[4,512,256]{2,1,0:T(8,128)(2,1)S(1)} %get-tuple-element.9.high_ref, bf16[4,512,256]{2,1,0:T(8,128)(2,1)S(1)} %get-tuple-element.10.low_ref, f32[8,24,128]{2,1,0:T(8,128)S(1)} %all-to-all-done.block_ref), custom_call_target="tpu_custom_call" | custom-call | tf_op jit(solution)/shard_map/contract/pallas_call | solution.py:199
  12.6 2.0 %all-gather = f32[512,128]{1,0:T(8,128)S(1)} all-gather(f32[256,128]{1,0:T(8,128)S(1)} %get-tuple-element.11), channel_id=2, replica_groups=mesh['ia'=4,'ja'=16,'x'=4,'c'=2] {'c'}, dimensions={0}, use_global_device_ids=true | all-gather | bytes 393216 | tf_op jit(solution)/shard_map/all_gather | solution.py:206
  14.6 0.1 compose.1
  14.7 23.3 %all_to_all.10 = f32[64,1,896]{2,1,0:T(1,128)S(1)} all-to-all(f32[64,1,896]{2,1,0:T(1,128)S(1)} %bitcast.5), channel_id=1, replica_groups=mesh['ia'=4,'ja'=16,'x'=4,'c'=2] {'ja','x'}, dimensions={0} | all-to-all | bytes 458752 | tf_op jit(solution)/shard_map/all_to_all | solution.py:210
  38.0 2.1 %solve.1 = f32[4,64]{1,0:T(4,128)} custom-call(f32[448,128]{1,0:T(8,128)S(1)} %bitcast.4), custom_call_target="tpu_custom_call" | custom-call | tf_op jit(solution)/shard_map/solve/pallas_call | solution.py:211
Async XLA Ops:
  1.5 10.1 %all-to-all-start = ((f32[8,24,128]{2,1,0:T(8,128)}), f32[8,24,128]{2,1,0:T(8,128)S(1)}, u32[]{:S(2)}, u32[]{:S(2)}) async-start(f32[8,24,128]{2,1,0:T(8,128)} %spread.1), calls=%async_computation | async-start | bytes 196608 | tf_op jit(solution)/shard_map/all_to_all | solution.py:198
  5.8 1.6 %copy-start = (f32[4,512,256]{2,1,0:T(8,128)S(1)}, f32[4,512,256]{2,1,0:T(8,128)}, u32[]{:S(2)}) copy-start(f32[4,512,256]{2,1,0:T(8,128)} %t_ref.1) | copy-start | bytes 6291460

commit v6 on v5

--- a/solution.py
+++ b/solution.py
@@ -19,13 +19,14 @@
         copy.start()
     for copy in copies:
         copy.wait()
-    rows, rank = b_own.shape
+    rows = b_own.shape[0]
+    depth = c_own.shape[0]
     b = jnp.concatenate([b_own[: rows // 2], b_own[rows // 2 :]], axis=1)
-    c = jnp.concatenate([c_own[...], jnp.zeros((8 - c_own.shape[0], rank), F32)], axis=0)
-    c = jnp.concatenate([c, c], axis=1)
+    c = jnp.concatenate([c_own[: depth // 2], c_own[depth // 2 :]], axis=1)
+    lines = (rows + depth) // 2
     for peer in range(n_ka):
-        out_ref[peer, : rows // 2] = b
-        out_ref[peer, rows // 2 :] = c
+        out_ref[lines * peer : lines * peer + rows // 2] = b
+        out_ref[lines * peer + rows // 2 : lines * (peer + 1)] = c
 
 
 def split(x):
@@ -46,36 +47,37 @@
     x = lax.axis_index("x")
     ka = x * lax.axis_size("c") + lax.axis_index("c")
     depth, rows, cols = high_ref.shape
-    rank = block_ref.shape[2] // 2
-    wide = 2 * rank
-    b = jnp.concatenate([block_ref[:, :-8, :rank], block_ref[:, :-8, rank:]], axis=1).reshape(-1, rank)
-    c_wide = block_ref[:, -8:].reshape(-1, wide)
-    gram_ref[...] = transposed_dot(b, jnp.concatenate([b, b], axis=1)) * transposed_dot(c_wide[:, :rank], c_wide)
-    nothing = jnp.zeros(b.shape, B16)
+    wide = block_ref.shape[1]
+    rank = wide // 2
+    n_ka = lax.axis_size("x") * lax.axis_size("c")
+    lines = block_ref.shape[0] // n_ka
+    b_lines = lines - depth // 2
+    b = [block_ref[lines * peer : lines * peer + b_lines, :] for peer in range(n_ka)]
+    b = jnp.concatenate([part[:, at : at + rank] for part in b for at in (0, rank)], axis=0)
+    c_lines = [block_ref[pl.ds(b_lines + k, n_ka, stride=lines), :] for k in range(depth // 2)]
+    c_lines = jnp.concatenate(c_lines + [pltpu.roll(line, rank, 1) for line in c_lines], axis=0)
+    c_wide = jnp.concatenate([c_lines[:, :rank]] * 2, axis=1)
+    b_wide = jnp.concatenate([b, b], axis=1)
+    gram_ref[...] = transposed_dot(b, b_wide) * transposed_dot(c_wide[:, :rank], c_wide)
+    column = lax.broadcasted_iota(jnp.int32, b_wide.shape, 1)
     weights = []
     for k in range(depth):
-        high, low = split(b * block_ref[ka, pl.ds(block_ref.shape[1] - 8 + k, 1), :rank])
-        weights.append(
-            (
-                jnp.concatenate([high, low], axis=1),
-                jnp.concatenate([high, nothing], axis=1),
-                jnp.concatenate([low, high], axis=1),
-                jnp.concatenate([nothing, high], axis=1),
-            )
-        )
-    step = rows // 4
-    lane = lax.broadcasted_iota(jnp.int32, (step, wide), 1)
-    for at in range(0, rows // 2, step):
-        sides = []
-        for side in range(2):
-            start = at + side * (rows // 2)
-            first = jnp.zeros((step, wide), F32)
-            second = jnp.zeros((step, wide), F32)
-            for k in range(depth):
-                first += jnp.dot(high_ref[k, start : start + step, :], weights[k][2 * side], preferred_element_type=F32)
-                second += jnp.dot(low_ref[k, start : start + step, :], weights[k][2 * side + 1], preferred_element_type=F32)
-            sides.append(first + (pltpu.roll(first, rank, 1) + second))
-        sums_ref[at : at + step, :] = jnp.where(lane < rank, sides[0], sides[1])
+        c_own = block_ref[pl.ds(lines * ka + b_lines + k % (depth // 2), 1), :]
+        turned = pltpu.roll(c_own, rank, 1)
+        c_own = jnp.where((column[:1] < rank) == (k < depth // 2), c_own, turned)
+        scaled = b_wide * c_own
+        high = scaled.astype(B16)
+        rounded = high.astype(F32)
+        weights.append((jnp.where(column < rank, rounded, scaled - rounded).astype(B16), high))
+    first = jnp.zeros((rows, wide), F32)
+    for k in range(depth):
+        first += jnp.dot(high_ref[k], weights[k][0], preferred_element_type=F32)
+    second = jnp.zeros((rows, wide), F32)
+    for k in range(depth):
+        second += jnp.dot(low_ref[k], weights[k][1], preferred_element_type=F32)
+    sums = first + (pltpu.roll(first, rank, 1) + second)
+    lane = lax.broadcasted_iota(jnp.int32, (rows // 2, wide), 1)
+    sums_ref[...] = jnp.where(lane < rank, sums[: rows // 2], sums[rows // 2 :])
     own = gram_ref[pl.ds(x, 16, stride=4), :]
     by16, by80, by96 = (pltpu.roll(own, n, 1) for n in (16, 80, 96))
     lane = lax.broadcasted_iota(jnp.int32, (1, wide), 1)
@@ -143,14 +145,19 @@
     def row(a, r):
         return jnp.take_along_axis(a, jnp.full((8, wide), r, jnp.int32), axis=0)
 
+    rows = [row(groups[0], s) for s in range(8)]
     for r in range(8):
         at = rank + 8 * r
         later = range(r + 1, 9)
-        rows = [row(groups[r], s) for s in range(8)]
         pivots = {(u, v): column(rows[u], at + v) for u in range(8) for v in range(u + 1)}
         left = {g: [column(groups[g], at + s) for s in range(8)] for g in later}
         terms = {g: [] for g in later}
+        following = None
         for t in range(8):
+            if t == 6 and r < 7:
+                for term in terms[r + 1]:
+                    groups[r + 1] = groups[r + 1] - term
+                following = [row(groups[r + 1], s) for s in range(8)]
             inv = 1.0 / pivots[t, t]
             scaled = rows[t] * inv
             ratio = {u: pivots[u, t] * inv for u in range(t + 1, 8)}
@@ -159,12 +166,17 @@
                     pivots[u, v] = pivots[u, v] - ratio[u] * pivots[v, t]
                 rows[u] = rows[u] - ratio[u] * rows[t]
             for g in later:
-                terms[g].append(left[g][t] * scaled)
+                if following is not None and g == r + 1:
+                    following = [following[s] - row(left[g][t], s) * scaled for s in range(8)]
+                else:
+                    terms[g].append(left[g][t] * scaled)
                 for u in range(t + 1, 8):
                     left[g][u] = left[g][u] - ratio[u] * left[g][t]
         for g in later:
-            head, tail = terms[g][:4], terms[g][4:]
-            groups[g] = groups[g] - (total(head) + (total(tail[:2]) + tail[2]) + tail[3])
+            if following is None or g > r + 1:
+                head, tail = terms[g][:4], terms[g][4:]
+                groups[g] = groups[g] - (total(head) + (total(tail[:2]) + tail[2]) + tail[3])
+        rows = following
     out_ref[...] = -groups[8][: out_ref.shape[0], :rank]
 
 
@@ -177,9 +189,10 @@
     n_ka = n_x * n_c
     rows_b, rank = factor_b.shape
     rows = tensor.shape[1]
+    lines = (rows_b + factor_c.shape[0]) // 2
     mine = pl.pallas_call(
         functools.partial(spread, n_ka),
-        out_shape=array(n_ka, rows_b // 2 + 8, 2 * rank),
+        out_shape=array(n_ka * lines, 2 * rank),
         in_specs=[pl.BlockSpec(memory_space=pl.ANY)] * 2,
         scratch_shapes=[
             pltpu.VMEM(factor_b.shape, F32),
@@ -195,14 +208,14 @@
         cost_estimate=pl.CostEstimate(flops=2**21, bytes_accessed=2**22, transcendentals=0),
         name="halve",
     )(tensor)
-    block = lax.all_to_all(mine, ("x", "c"), 0, 0, tiled=True)
+    block = lax.all_to_all(mine.reshape(n_ka, 1, lines * 2 * rank), ("x", "c"), 0, 0, tiled=True)
     sums, piece = pl.pallas_call(
         contract,
         out_shape=[array(rows // 2, 2 * rank), array(8, 2 * rank)],
         scratch_shapes=[pltpu.VMEM((rank, 2 * rank), F32)],
         compiler_params=BIG,
         name="contract",
-    )(high, low, block)
+    )(high, low, block.reshape(n_ka * lines, 2 * rank))
     both = lax.all_gather(sums, "c")
     packed = pl.pallas_call(
         compose, out_shape=array(n_ja * n_x * 7, 2 * rank), compiler_params=BIG, name="compose"

time: 40.4 us -> 40.3 us (level)
  no operation moved by 1% of the time
where the time goes in v6:
time: 40.3 us; the launch traced here: 39.9 us
  blocking collectives  25.3 us (63%)
  Pallas kernels  4.99 us (12%)
  starting transfers between devices  4.31 us (11%)
  waiting for transfers between devices  3.7 us (9%)
  local copies, waits for them, and re-layouts  1.59 us (4%)
    all_to_all x1, blocking collectives, per_device(): lax.all_to_all(packed.reshape(n_ja * n_x, 1, 14 * rank), ('ja', 'x'), 0,...  23.3 us
    all_to_all x1, starting transfers between devices, per_device(): lax.all_to_all(mine.reshape(n_ka, 1, lines * 2 * rank), ('x', 'c'), 0, 0,...  4.31 us
    all_to_all x1, waiting for transfers between devices, per_device(): lax.all_to_all(mine.reshape(n_ka, 1, lines * 2 * rank), ('x', 'c'), 0, 0,...  3.7 us
    pallas_call x1, Pallas kernels, per_device(): pl.pallas_call(functools.partial(solve, n_x), out_shape=array(rows // (n_...  2.04 us
    all_gather x1, blocking collectives, per_device(): both = lax.all_gather(sums, 'c')  1.99 us
    unnamed x2, local copies, waits for them, and re-layouts  1.59 us
    pallas_call x1, Pallas kernels, per_device(): pl.pallas_call(functools.partial(spread, n_ka), out_shape=array(n_ka * li...  1.43 us
    pallas_call x1, Pallas kernels, per_device(): pl.pallas_call(contract, out_shape=[array(rows // 2, 2 * rank), array(8,...  1.05 us
  transfers between devices with their start and end apart: 1, of which 1 were waited for; matrix products, arithmetic and copies ran while one was open for 0% of the time, Pallas kernels for 1%

profile of v6, /device:TPU:128, one launch (start us, length us, event | category | flops | bytes accessed | tf_op | source)
XLA Modules:
  0.0 39.9 jit_solution(14334652620110405695)
XLA Ops:
  0.0 1.4 %spread.1 = f32[144,128]{1,0:T(8,128)} custom-call(f32[32,64]{1,0:T(8,128)} %b_ref.1, f32[4,64]{1,0:T(4,128)} %c_ref.1), custom_call_target="tpu_custom_call" | custom-call | tf_op jit(solution)/shard_map/spread/pallas_call | solution.py:193
  1.4 4.3 %all-to-all-start = ((f32[8,1,2304]{2,1,0:T(1,128)}), f32[8,1,2304]{2,1,0:T(1,128)S(1)}, u32[]{:S(2)}, u32[]{:S(2)}) async-start(f32[8,1,2304]{2,1,0:T(1,128)} %bitcast.9), calls=%async_computation | async-start | bytes 147456 | tf_op jit(solution)/shard_map/all_to_all | solution.py:211
  5.7 0.0 copy-start
  5.8 1.6 %copy-done = f32[4,512,256]{2,1,0:T(8,128)S(1)} copy-done((f32[4,512,256]{2,1,0:T(8,128)S(1)}, f32[4,512,256]{2,1,0:T(8,128)}, u32[]{:S(2)}) %copy-start) | copy-done | bytes 2097176
  7.3 0.4 halve.1
  7.7 3.7 %all-to-all-done = f32[8,1,2304]{2,1,0:T(1,128)S(1)} async-done(((f32[8,1,2304]{2,1,0:T(1,128)}), f32[8,1,2304]{2,1,0:T(1,128)S(1)}, u32[]{:S(2)}, u32[]{:S(2)}) %all-to-all-start) | async-done | bytes 73760 | tf_op jit(solution)/shard_map/all_to_all | solution.py:211
  11.4 1.0 %contract.1 = (f32[256,128]{1,0:T(8,128)S(1)}, f32[8,128]{1,0:T(8,128)S(1)}) custom-call(bf16[4,512,256]{2,1,0:T(8,128)(2,1)S(1)} %get-tuple-element.9.high_ref, bf16[4,512,256]{2,1,0:T(8,128)(2,1)S(1)} %get-tuple-element.10.low_ref, f32[144,128]{1,0:T(8,128)S(1)} %bitcast.8), custom_call_target="tpu_custom_call" | custom-call | tf_op jit(solution)/shard_map/contract/pallas_call | solution.py:212
  12.5 2.0 %all-gather = f32[512,128]{1,0:T(8,128)S(1)} all-gather(f32[256,128]{1,0:T(8,128)S(1)} %get-tuple-element.11), channel_id=2, replica_groups=mesh['ia'=4,'ja'=16,'x'=4,'c'=2] {'c'}, dimensions={0}, use_global_device_ids=true | all-gather | bytes 393216 | tf_op jit(solution)/shard_map/all_gather | solution.py:219
  14.5 0.1 compose.1
  14.6 23.3 %all_to_all.10 = f32[64,1,896]{2,1,0:T(1,128)S(1)} all-to-all(f32[64,1,896]{2,1,0:T(1,128)S(1)} %bitcast.7), channel_id=1, replica_groups=mesh['ia'=4,'ja'=16,'x'=4,'c'=2] {'ja','x'}, dimensions={0} | all-to-all | bytes 458752 | tf_op jit(solution)/shard_map/all_to_all | solution.py:223
  37.9 2.0 %solve.1 = f32[4,64]{1,0:T(4,128)} custom-call(f32[448,128]{1,0:T(8,128)S(1)} %bitcast.6), custom_call_target="tpu_custom_call" | custom-call | tf_op jit(solution)/shard_map/solve/pallas_call | solution.py:224
Async XLA Ops:
  1.4 10.0 %all-to-all-start = ((f32[8,1,2304]{2,1,0:T(1,128)}), f32[8,1,2304]{2,1,0:T(1,128)S(1)}, u32[]{:S(2)}, u32[]{:S(2)}) async-start(f32[8,1,2304]{2,1,0:T(1,128)} %bitcast.9), calls=%async_computation | async-start | bytes 147456 | tf_op jit(solution)/shard_map/all_to_all | solution.py:211
  5.7 1.6 %copy-start = (f32[4,512,256]{2,1,0:T(8,128)S(1)}, f32[4,512,256]{2,1,0:T(8,128)}, u32[]{:S(2)}) copy-start(f32[4,512,256]{2,1,0:T(8,128)} %t_ref.1) | copy-start | bytes 6291460

commit v7 on v5

--- a/solution.py
+++ b/solution.py
@@ -50,32 +50,24 @@
     wide = 2 * rank
     b = jnp.concatenate([block_ref[:, :-8, :rank], block_ref[:, :-8, rank:]], axis=1).reshape(-1, rank)
     c_wide = block_ref[:, -8:].reshape(-1, wide)
-    gram_ref[...] = transposed_dot(b, jnp.concatenate([b, b], axis=1)) * transposed_dot(c_wide[:, :rank], c_wide)
-    nothing = jnp.zeros(b.shape, B16)
+    b_wide = jnp.concatenate([b, b], axis=1)
+    gram_ref[...] = transposed_dot(b, b_wide) * transposed_dot(c_wide[:, :rank], c_wide)
+    column = lax.broadcasted_iota(jnp.int32, b_wide.shape, 1)
     weights = []
     for k in range(depth):
-        high, low = split(b * block_ref[ka, pl.ds(block_ref.shape[1] - 8 + k, 1), :rank])
-        weights.append(
-            (
-                jnp.concatenate([high, low], axis=1),
-                jnp.concatenate([high, nothing], axis=1),
-                jnp.concatenate([low, high], axis=1),
-                jnp.concatenate([nothing, high], axis=1),
-            )
-        )
-    step = rows // 4
-    lane = lax.broadcasted_iota(jnp.int32, (step, wide), 1)
-    for at in range(0, rows // 2, step):
-        sides = []
-        for side in range(2):
-            start = at + side * (rows // 2)
-            first = jnp.zeros((step, wide), F32)
-            second = jnp.zeros((step, wide), F32)
-            for k in range(depth):
-                first += jnp.dot(high_ref[k, start : start + step, :], weights[k][2 * side], preferred_element_type=F32)
-                second += jnp.dot(low_ref[k, start : start + step, :], weights[k][2 * side + 1], preferred_element_type=F32)
-            sides.append(first + (pltpu.roll(first, rank, 1) + second))
-        sums_ref[at : at + step, :] = jnp.where(lane < rank, sides[0], sides[1])
+        scaled = b_wide * block_ref[ka, pl.ds(block_ref.shape[1] - 8 + k, 1), :]
+        high = scaled.astype(B16)
+        rounded = high.astype(F32)
+        weights.append((jnp.where(column < rank, rounded, scaled - rounded).astype(B16), high))
+    first = jnp.zeros((rows, wide), F32)
+    for k in range(depth):
+        first += jnp.dot(high_ref[k], weights[k][0], preferred_element_type=F32)
+    second = jnp.zeros((rows, wide), F32)
+    for k in range(depth):
+        second += jnp.dot(low_ref[k], weights[k][1], preferred_element_type=F32)
+    sums = first + (pltpu.roll(first, rank, 1) + second)
+    lane = lax.broadcasted_iota(jnp.int32, (rows // 2, wide), 1)
+    sums_ref[...] = jnp.where(lane < rank, sums[: rows // 2], sums[rows // 2 :])
     own = gram_ref[pl.ds(x, 16, stride=4), :]
     by16, by80, by96 = (pltpu.roll(own, n, 1) for n in (16, 80, 96))
     lane = lax.broadcasted_iota(jnp.int32, (1, wide), 1)

time: 40.4 us -> 40.4 us (level)
  no operation moved by 1% of the time
where the time goes in v7:
time: 40.4 us; the launch traced here: 40.1 us
  blocking collectives  25.3 us (63%)
  Pallas kernels  4.99 us (12%)
  starting transfers between devices  4.31 us (11%)
  waiting for transfers between devices  3.83 us (9%)
  local copies, waits for them, and re-layouts  1.59 us (4%)
    all_to_all x1, blocking collectives, per_device(): lax.all_to_all(packed.reshape(n_ja * n_x, 1, 14 * rank), ('ja', 'x'), 0,...  23.3 us
    all_to_all x1, starting transfers between devices, per_device(): block = lax.all_to_all(mine, ('x', 'c'), 0, 0, tiled=True)  4.31 us
    all_to_all x1, waiting for transfers between devices, per_device(): block = lax.all_to_all(mine, ('x', 'c'), 0, 0, tiled=True)  3.83 us
    pallas_call x1, Pallas kernels, per_device(): pl.pallas_call(functools.partial(solve, n_x), out_shape=array(rows // (n_...  2.06 us
    all_gather x1, blocking collectives, per_device(): both = lax.all_gather(sums, 'c')  1.99 us
    unnamed x2, local copies, waits for them, and re-layouts  1.59 us
    pallas_call x1, Pallas kernels, per_device(): pl.pallas_call(functools.partial(spread, n_ka), out_shape=array(n_ka, row...  1.45 us
    pallas_call x1, Pallas kernels, per_device(): pl.pallas_call(contract, out_shape=[array(rows // 2, 2 * rank), array(8,...  1 us
  transfers between devices with their start and end apart: 1, of which 1 were waited for; matrix products, arithmetic and copies ran while one was open for 0% of the time, Pallas kernels for 1%

profile of v7, /device:TPU:128, one launch (start us, length us, event | category | flops | bytes accessed | tf_op | source)
XLA Modules:
  0.0 40.1 jit_solution(16861213458980761096)
XLA Ops:
  0.0 1.4 %spread.1 = f32[8,24,128]{2,1,0:T(8,128)} custom-call(f32[32,64]{1,0:T(8,128)} %b_ref.1, f32[4,64]{1,0:T(4,128)} %c_ref.1), custom_call_target="tpu_custom_call" | custom-call | tf_op jit(solution)/shard_map/spread/pallas_call | solution.py:172
  1.5 4.3 %all-to-all-start = ((f32[8,24,128]{2,1,0:T(8,128)}), f32[8,24,128]{2,1,0:T(8,128)S(1)}, u32[]{:S(2)}, u32[]{:S(2)}) async-start(f32[8,24,128]{2,1,0:T(8,128)} %spread.1), calls=%async_computation | async-start | bytes 196608 | tf_op jit(solution)/shard_map/all_to_all | solution.py:190
  5.8 0.0 copy-start
  5.8 1.6 %copy-done = f32[4,512,256]{2,1,0:T(8,128)S(1)} copy-done((f32[4,512,256]{2,1,0:T(8,128)S(1)}, f32[4,512,256]{2,1,0:T(8,128)}, u32[]{:S(2)}) %copy-start) | copy-done | bytes 2097176
  7.4 0.4 halve.1
  7.7 3.8 %all-to-all-done.block_ref = f32[8,24,128]{2,1,0:T(8,128)S(1)} async-done(((f32[8,24,128]{2,1,0:T(8,128)}), f32[8,24,128]{2,1,0:T(8,128)S(1)}, u32[]{:S(2)}, u32[]{:S(2)}) %all-to-all-start) | async-done | bytes 98336 | tf_op jit(solution)/shard_map/all_to_all | solution.py:190
  11.6 1.0 %contract.1 = (f32[256,128]{1,0:T(8,128)S(1)}, f32[8,128]{1,0:T(8,128)S(1)}) custom-call(bf16[4,512,256]{2,1,0:T(8,128)(2,1)S(1)} %get-tuple-element.9.high_ref, bf16[4,512,256]{2,1,0:T(8,128)(2,1)S(1)} %get-tuple-element.10.low_ref, f32[8,24,128]{2,1,0:T(8,128)S(1)} %all-to-all-done.block_ref), custom_call_target="tpu_custom_call" | custom-call | tf_op jit(solution)/shard_map/contract/pallas_call | solution.py:191
  12.6 2.0 %all-gather = f32[512,128]{1,0:T(8,128)S(1)} all-gather(f32[256,128]{1,0:T(8,128)S(1)} %get-tuple-element.11), channel_id=2, replica_groups=mesh['ia'=4,'ja'=16,'x'=4,'c'=2] {'c'}, dimensions={0}, use_global_device_ids=true | all-gather | bytes 393216 | tf_op jit(solution)/shard_map/all_gather | solution.py:198
  14.6 0.1 compose.1
  14.7 23.3 %all_to_all.10 = f32[64,1,896]{2,1,0:T(1,128)S(1)} all-to-all(f32[64,1,896]{2,1,0:T(1,128)S(1)} %bitcast.5), channel_id=1, replica_groups=mesh['ia'=4,'ja'=16,'x'=4,'c'=2] {'ja','x'}, dimensions={0} | all-to-all | bytes 458752 | tf_op jit(solution)/shard_map/all_to_all | solution.py:202
  38.0 2.1 %solve.1 = f32[4,64]{1,0:T(4,128)} custom-call(f32[448,128]{1,0:T(8,128)S(1)} %bitcast.4), custom_call_target="tpu_custom_call" | custom-call | tf_op jit(solution)/shard_map/solve/pallas_call | solution.py:203
Async XLA Ops:
  1.5 10.1 %all-to-all-start = ((f32[8,24,128]{2,1,0:T(8,128)}), f32[8,24,128]{2,1,0:T(8,128)S(1)}, u32[]{:S(2)}, u32[]{:S(2)}) async-start(f32[8,24,128]{2,1,0:T(8,128)} %spread.1), calls=%async_computation | async-start | bytes 196608 | tf_op jit(solution)/shard_map/all_to_all | solution.py:190
  5.8 1.6 %copy-start = (f32[4,512,256]{2,1,0:T(8,128)S(1)}, f32[4,512,256]{2,1,0:T(8,128)}, u32[]{:S(2)}) copy-start(f32[4,512,256]{2,1,0:T(8,128)} %t_ref.1) | copy-start | bytes 6291460
